TPU v7x, 32 devices: a whole 2x2x4 slice. The times are simulated.
32 devices in a mesh: groups: 2 (over x), layer: 16 (over z, y, core).
Axes of the slice: x: 2, y: 2, z: 4, core: 2. Of those that a mesh axis runs over, the one named last changes fastest.
Arguments:
- queries: bfloat16 [128, 32, 1024], P('groups', 'layer'), parts along dimension 0, may hold values from -6 to 6
- inverse_curvature: float32 [32, 1024], P('layer'), may hold values from 0.25 to 4
- store: bfloat16 [64, 32, 1024], P(('groups', 'layer')), parts along dimension 0, may hold values from -6 to 6
- exponents: int32 [64, 32], P(('groups', 'layer')), parts along dimension 0, may hold values from -3 to 1, as said below
Outputs:
- scores: float32 [128, 32], P(('groups', 'layer')), parts along dimension 0
There are 2 independent parts, one for each index of `groups`. A program takes and returns all parts, laid end to end along the dimension named above; an argument that names none is the same for every part. Nothing has to cross between parts.
Inputs may be any that keep to these rules, and one draw needn't show every extreme that they name: `exponents`: exponents of the first half of the matrices lie in -3 to 0, those of the second half in -2 to 1.
All inputs are finite; a program needn't handle non-finite values.
Results may differ from a plain program's by a relative error of at most 0.0029.
Values may be sent and summed in bfloat16 or wider, within the bound.
A program may use at most 64 MiB of HBM per device.

v0:
```python
import jax
import jax.numpy as jnp
from jax import lax
from jax.sharding import PartitionSpec as P


def local(queries, inverse_curvature, store, exponents):
    layers = lax.axis_size("layer")
    ex_dev, mats, feat = store.shape
    count_q = queries.shape[0]
    mat_dev = queries.shape[1]
    width = mat_dev * feat
    weighted = (queries.astype(jnp.float32) * inverse_curvature[None, :, :]).astype(jnp.bfloat16)
    weighted = weighted.reshape(count_q, width)
    blocks = store.reshape(1, ex_dev, layers, width)
    scales = exponents.reshape(1, ex_dev, layers, mat_dev)
    values = lax.all_to_all(blocks, "layer", split_axis=2, concat_axis=0, tiled=True)
    codes = lax.all_to_all(scales, "layer", split_axis=2, concat_axis=0, tiled=True)
    sources = values.shape[0]
    items = values.shape[1]
    factor = jnp.exp2(codes.astype(jnp.float32)).reshape(sources, items, mat_dev, 1)
    grid = values.astype(jnp.float32).reshape(sources, items, mat_dev, feat) * factor
    decoded = grid.astype(jnp.bfloat16).reshape(sources, items, width)
    partial_value = jnp.sum(jnp.square(decoded.astype(jnp.float32)), axis=2)
    moved = (decoded, partial_value)
    decoded, partial_value = moved
    rows_all = decoded.reshape(layers * ex_dev, width)
    norms = lax.psum(partial_value.reshape(layers * ex_dev), "layer")
    mine = lax.psum_scatter(
        lax.dot_general(
            weighted, rows_all, (((1,), (1,)), ((), ())), preferred_element_type=jnp.float32
        ),
        "layer",
        scatter_dimension=0,
        tiled=True,
    )
    return mine / jnp.sqrt(norms + 1e-06)[None, :]


def solution(mesh):
    return jax.shard_map(
        local,
        mesh=mesh,
        in_specs=(
            P("groups", "layer", None),
            P("layer", None),
            P(("groups", "layer"), None, None),
            P(("groups", "layer"), None),
        ),
        out_specs=P(("groups", "layer"), None),
        check_vma=False,
    )
```

profile of v0, /device:TPU:0, one launch (start us, length us, event | category | flops | bytes accessed | tf_op | source)
XLA Modules:
  0.0 86.6 jit_solution(11338867171957640970)
XLA Ops:
  0.0 0.8 reshape.70
  0.8 0.6 copy.24
  1.4 7.4 %all-to-all-start.1 = ((s32[1,2,16,2]{3,1,0,2:T(2,128)}), s32[1,2,16,2]{3,1,0,2:T(2,128)S(1)}, u32[]{:S(2)}, u32[]{:S(2)}) async-start(s32[1,2,16,2]{3,1,0,2:T(2,128)} %copy.24), calls=%async_computation.1 | async-start | bytes 32768 | tf_op jit(solution)/shard_map/all_to_all | solution.py:18
  8.8 1.0 %reshape.69 = bf16[1,2,16,2048]{3,2,1,0:T(8,128)(2,1)S(1)} reshape(bf16[2,32,1024]{2,1,0:T(8,128)(2,1)} %param.6) | data formatting | bytes 262144 | tf_op jit(solution)/shard_map/reshape | solution.py:15
  9.7 0.0 copy-start
  9.7 0.8 copy.22
  10.5 0.0 copy-start.1
  10.5 4.7 %all-to-all-done.1 = s32[1,2,16,2]{3,1,0,2:T(2,128)S(1)} async-done(((s32[1,2,16,2]{3,1,0,2:T(2,128)}), s32[1,2,16,2]{3,1,0,2:T(2,128)S(1)}, u32[]{:S(2)}, u32[]{:S(2)}) %all-to-all-start.1) | async-done | bytes 288 | tf_op jit(solution)/shard_map/all_to_all | solution.py:18
  15.3 3.5 %all-to-all-start = ((bf16[1,2,16,2048]{3,1,0,2:T(2,128)(2,1)}), bf16[1,2,16,2048]{3,1,0,2:T(2,128)(2,1)S(1)}, u32[]{:S(2)}, u32[]{:S(2)}) async-start(bf16[1,2,16,2048]{3,1,0,2:T(2,128)(2,1)} %copy.22), calls=%async_computation | async-start | bytes 262144 | tf_op jit(solution)/shard_map/all_to_all | solution.py:17
  18.8 0.0 copy-done
  18.8 0.0 copy-done.1
  18.8 0.2 multiply_convert_fusion
  19.0 0.1 copy.32
  19.1 0.0 copy-start.2
  19.1 0.6 copy-done.2
  19.8 0.6 dynamic-slice
  21.0 0.1 copy.25
  21.1 0.1 copy.26
  21.2 0.1 mul.33
  21.3 0.3 reshape.76
  21.7 5.0 %all-to-all-done = bf16[1,2,16,2048]{3,1,0,2:T(2,128)(2,1)S(1)} async-done(((bf16[1,2,16,2048]{3,1,0,2:T(2,128)(2,1)}), bf16[1,2,16,2048]{3,1,0,2:T(2,128)(2,1)S(1)}, u32[]{:S(2)}, u32[]{:S(2)}) %all-to-all-start) | async-done | bytes 131104 | tf_op jit(solution)/shard_map/all_to_all | solution.py:17
  26.7 0.2 reshape.72
  27.0 0.2 fusion.1
  27.2 0.3 bitcast_reduce_fusion
  27.4 0.1 copy.30
  27.5 0.1 reshape.71
  27.6 0.2 fusion.2
  27.8 58.2 %all-reduce.1 = (f32[64,32]{1,0:T(8,128)S(1)}, f32[32]{0:T(128)S(1)}) all-reduce(f32[64,32]{1,0:T(8,128)S(1)} %fusion.2, f32[32]{0:T(128)S(1)} %reshape.71), channel_id=2, replica_groups=mesh['groups'=2,'layer'=16] {'layer'}, use_global_device_ids=true, to_apply=%region_0.0.clone | all-reduce | flops 2080 | bytes 16640
  86.0 0.6 dynamic-slice_divide_fusion
  (4 shorter events, 0.1 us)
Async XLA Ops:
  1.4 13.9 %all-to-all-start.1 = ((s32[1,2,16,2]{3,1,0,2:T(2,128)}), s32[1,2,16,2]{3,1,0,2:T(2,128)S(1)}, u32[]{:S(2)}, u32[]{:S(2)}) async-start(s32[1,2,16,2]{3,1,0,2:T(2,128)} %copy.24), calls=%async_computation.1 | async-start | bytes 32768 | tf_op jit(solution)/shard_map/all_to_all | solution.py:18
  9.7 9.1 %copy-start = (bf16[64,2,1024]{2,1,0:T(2,128)(2,1)S(1)}, bf16[64,2,1024]{2,1,0:T(2,128)(2,1)}, u32[]{:S(2)}) copy-start(bf16[64,2,1024]{2,1,0:T(2,128)(2,1)} %param.4) | copy-start | bytes 786436
  10.5 8.3 %copy-start.1 = (f32[2,1024]{1,0:T(2,128)S(1)}, f32[2,1024]{1,0:T(2,128)}, u32[]{:S(2)}) copy-start(f32[2,1024]{1,0:T(2,128)} %param.5) | copy-start | bytes 24580
  15.3 11.4 %all-to-all-start = ((bf16[1,2,16,2048]{3,1,0,2:T(2,128)(2,1)}), bf16[1,2,16,2048]{3,1,0,2:T(2,128)(2,1)S(1)}, u32[]{:S(2)}, u32[]{:S(2)}) async-start(bf16[1,2,16,2048]{3,1,0,2:T(2,128)(2,1)} %copy.22), calls=%async_computation | async-start | bytes 262144 | tf_op jit(solution)/shard_map/all_to_all | solution.py:17
  19.1 0.7 copy-start.2
where the time goes:
time: 86.9 us; the launch traced here: 86.6 us
  blocking collectives  58.2 us (67%)
  starting transfers between devices  10.9 us (13%)
  waiting for transfers between devices  9.77 us (11%)
  local copies, waits for them, and re-layouts  5.48 us (6%)
  other arithmetic  1.28 us (1%)
    unnamed x1, blocking collectives  58.2 us
    all_to_all x1, starting transfers between devices, local(): lax.all_to_all(scales, 'layer', split_axis=2, concat_axis=0, tiled=True)  7.39 us
    all_to_all x1, waiting for transfers between devices, local(): lax.all_to_all(blocks, 'layer', split_axis=2, concat_axis=0, tiled=True)  5.03 us
    all_to_all x1, waiting for transfers between devices, local(): lax.all_to_all(scales, 'layer', split_axis=2, concat_axis=0, tiled=True)  4.74 us
    all_to_all x1, starting transfers between devices, local(): lax.all_to_all(blocks, 'layer', split_axis=2, concat_axis=0, tiled=True)  3.51 us
  transfers between devices with their start and end apart: 2, of which 2 were waited for; matrix products, arithmetic and copies ran while one was open for 4% of the time, Pallas kernels for 0%

commit v1 on v0

v1 whole, which is shorter than its diff:
```python
import functools

import jax
import jax.numpy as jnp
from jax import lax
from jax.experimental import pallas as pl
from jax.experimental.pallas import tpu as pltpu
from jax.sharding import PartitionSpec as P

MESH = pl.DeviceIdType.MESH
ROWS = 16
QBLOCK = 64
SBLOCK = 16
MBLOCK = 32


def each(start, stop, body):
    if stop - start <= 16:
        for i in range(start, stop):
            body(i)
    else:
        lax.fori_loop(start, stop, lambda i, c: (body(i), c)[1], 0)


def iota(shape, axis):
    return lax.broadcasted_iota(jnp.int32, shape, axis)


def kernel(
    n,
    q_hbm,
    cur_hbm,
    st_hbm,
    exp_hbm,
    out_ref,
    q_ref,
    cur_ref,
    st_ref,
    exp_ref,
    flat,
    send,
    recv,
    weighted,
    part_send,
    part_recv,
    load_sem,
    send_sem,
    recv_sem,
    psend_sem,
    precv_sem,
):
    me = lax.axis_index("layer")
    ex, mats, feat = st_ref.shape
    count_q, mat_dev, _ = q_ref.shape
    chunks = ROWS // (ex * mat_dev)
    depth = feat // chunks
    sub = ex * chunks
    total = n * ex
    own_q = count_q // n
    lanes = part_send.shape[2]

    loads = [
        pltpu.make_async_copy(src, dst, load_sem.at[i])
        for i, (src, dst) in enumerate(
            [(exp_hbm, exp_ref), (st_hbm, st_ref), (cur_hbm, cur_ref), (q_hbm, q_ref)]
        )
    ]
    for load in loads:
        load.start()

    barrier = pltpu.get_barrier_semaphore()

    def greet(k):
        pl.semaphore_signal(
            barrier, inc=1, device_id={"layer": lax.rem(me + k, n)}, device_id_type=MESH
        )

    each(1, n, greet)

    loads[0].wait()
    loads[1].wait()
    factor_row = jnp.left_shift(1, exp_ref[...] + 3).astype(jnp.float32) * 0.125
    for first in range(0, mats, MBLOCK):
        pick = iota((MBLOCK, mats), 0) + first == iota((MBLOCK, mats), 1)
        for e in range(ex):
            row = jnp.broadcast_to(factor_row[e : e + 1, :], (MBLOCK, mats))
            factor = jnp.sum(jnp.where(pick, row, 0.0), axis=1, keepdims=True)
            grid = st_ref[e, pl.ds(first, MBLOCK), :].astype(jnp.float32) * factor
            for c in range(chunks):
                for t in range(depth // 128):
                    at = c * depth + t * 128
                    flat[t, pl.ds(first * sub + e * chunks + c, MBLOCK, stride=sub), :] = grid[
                        :, at : at + 128
                    ]
    for first in range(0, n, SBLOCK):
        size = min(SBLOCK, n - first)
        for t in range(depth // 128):
            rows = flat[t, pl.ds(first * ROWS, size * ROWS), :].astype(jnp.bfloat16)
            send[pl.ds(first, size), :, pl.ds(t * 128, 128)] = rows.reshape(size, ROWS, 128)

    pl.semaphore_wait(barrier, n - 1)

    def block_copy(peer, slot):
        return pltpu.make_async_remote_copy(
            src_ref=send.at[peer],
            dst_ref=recv.at[slot],
            send_sem=send_sem.at[peer],
            recv_sem=recv_sem.at[slot],
            device_id={"layer": peer},
            device_id_type=MESH,
        )

    def part_copy(peer, slot):
        return pltpu.make_async_remote_copy(
            src_ref=part_send.at[peer],
            dst_ref=part_recv.at[slot],
            send_sem=psend_sem.at[peer],
            recv_sem=precv_sem.at[slot],
            device_id={"layer": peer},
            device_id_type=MESH,
        )

    def peer_of(k):
        return lax.rem(me + k, n)

    each(1, n, lambda k: block_copy(peer_of(k), me).start())
    recv[me] = send[me]

    squares = jnp.zeros((sub, 128), jnp.float32)
    for t in range(depth // 128):
        values = flat[t].reshape(n * mat_dev, sub, 128)
        squares = squares + jnp.sum(values * values, axis=0)
    squares = jnp.sum(squares, axis=1, keepdims=True)
    spot = iota((sub, lanes), 1) == total + me * ex + iota((sub, lanes), 0) // chunks
    norm_row = jnp.sum(jnp.where(spot, squares, 0.0), axis=0, keepdims=True)

    loads[2].wait()
    loads[3].wait()

    def weigh(b):
        rows = pl.ds(b * QBLOCK, QBLOCK)
        grid = q_ref[rows].astype(jnp.float32) * cur_ref[...][None]
        for m in range(mat_dev):
            weighted[m, rows, :] = grid[:, m, :].astype(jnp.bfloat16)

    each(0, count_q // QBLOCK, weigh)

    each(1, n, lambda k: block_copy(peer_of(k), peer_of(k)).wait_recv())

    def score(b):
        rows = pl.ds(b * QBLOCK, QBLOCK)
        result = jnp.broadcast_to(norm_row, (QBLOCK, lanes))
        for first in range(0, n, SBLOCK):
            size = min(SBLOCK, n - first)
            width = size * ROWS
            blocks = recv[pl.ds(first, size)].reshape(width, depth)
            place = lax.rem(iota((QBLOCK, width), 1), ROWS)
            mix = jnp.zeros((QBLOCK, width), jnp.float32)
            for m in range(mat_dev):
                for c in range(chunks):
                    product = lax.dot_general(
                        weighted[m, rows, pl.ds(c * depth, depth)],
                        blocks,
                        (((1,), (1,)), ((), ())),
                        preferred_element_type=jnp.float32,
                    )
                    mine = (place // sub == m) & (lax.rem(place, chunks) == c)
                    mix = jnp.where(mine, product, mix)
            high = mix.astype(jnp.bfloat16)
            rest = mix - high.astype(jnp.float32)
            middle = rest.astype(jnp.bfloat16)
            low = (rest - middle.astype(jnp.float32)).astype(jnp.bfloat16)
            source = iota((width, lanes), 0)
            owner = (first + source // ROWS) * ex + lax.rem(source, sub) // chunks
            fold = jnp.where(owner == iota((width, lanes), 1), 1.0, 0.0).astype(jnp.bfloat16)
            for piece in (low, middle, high):
                result = result + jnp.dot(piece, fold, preferred_element_type=jnp.float32)
        for j in range(QBLOCK // own_q):
            part_send[b * (QBLOCK // own_q) + j] = result[j * own_q : (j + 1) * own_q, :]

    each(0, count_q // QBLOCK, score)

    each(1, n, lambda k: part_copy(peer_of(k), me).start())
    part_recv[me] = part_send[me]
    each(1, n, lambda k: part_copy(peer_of(k), peer_of(k)).wait_recv())
    final = jnp.sum(part_recv[...], axis=0)
    out_ref[...] = final[:, :total] / jnp.sqrt(final[:, total : 2 * total] + 1e-06)

    each(1, n, lambda k: block_copy(peer_of(k), me).wait_send())
    each(1, n, lambda k: part_copy(peer_of(k), me).wait_send())


def solution(mesh):
    n = mesh.shape["layer"]

    def local(queries, inverse_curvature, store, exponents):
        count_q, mat_dev, feat = queries.shape
        ex, mats, _ = store.shape
        chunks = ROWS // (ex * mat_dev)
        depth = feat // chunks
        total = n * ex
        own_q = count_q // n
        lanes = -(-2 * total // 128) * 128
        return pl.pallas_call(
            functools.partial(kernel, n),
            out_shape=jax.ShapeDtypeStruct((own_q, total), jnp.float32),
            in_specs=[pl.BlockSpec(memory_space=pl.ANY)] * 4,
            out_specs=pl.BlockSpec(memory_space=pltpu.VMEM),
            scratch_shapes=[
                pltpu.VMEM(queries.shape, queries.dtype),
                pltpu.VMEM(inverse_curvature.shape, inverse_curvature.dtype),
                pltpu.VMEM(store.shape, store.dtype),
                pltpu.VMEM(exponents.shape, exponents.dtype),
                pltpu.VMEM((depth // 128, n * ROWS, 128), jnp.float32),
                pltpu.VMEM((n, ROWS, depth), jnp.bfloat16),
                pltpu.VMEM((n, ROWS, depth), jnp.bfloat16),
                pltpu.VMEM((mat_dev, count_q, feat), jnp.bfloat16),
                pltpu.VMEM((n, own_q, lanes), jnp.float32),
                pltpu.VMEM((n, own_q, lanes), jnp.float32),
                pltpu.SemaphoreType.DMA((4,)),
                pltpu.SemaphoreType.DMA((n,)),
                pltpu.SemaphoreType.DMA((n,)),
                pltpu.SemaphoreType.DMA((n,)),
                pltpu.SemaphoreType.DMA((n,)),
            ],
            compiler_params=pltpu.CompilerParams(
                collective_id=0, has_side_effects=True, vmem_limit_bytes=32 * 1024 * 1024
            ),
        )(queries, inverse_curvature, store, exponents)

    return jax.shard_map(
        local,
        mesh=mesh,
        in_specs=(
            P("groups", "layer", None),
            P("layer", None),
            P(("groups", "layer"), None, None),
            P(("groups", "layer"), None),
        ),
        out_specs=P(("groups", "layer"), None),
        check_vma=False,
    )
```

time: 86.9 us -> 20.9 us (0.24)
  blocking collectives: 58.2 us -> 0 us
  Pallas kernels: 0 us -> 16.9 us
  starting transfers between devices: 10.9 us -> 0 us
  waiting for transfers between devices: 9.77 us -> 0 us
  local copies, waits for them, and re-layouts: 5.48 us -> 3.81 us
  other arithmetic: 1.28 us -> 0 us
    unnamed x1 -> x0, blocking collectives: 58.2 us -> none
    pallas_call x0 -> x1, Pallas kernels: none -> 16.9 us  [local(): pl.pallas_call(functools.partial(kernel, n), out_shape=jax.ShapeDtypeStru...]
    all_to_all x2 -> x0, starting transfers between devices: 10.9 us -> none  [the longest x1 7.39 us: local(): lax.all_to_all(scales, 'layer', split_axis=2, concat_axis=0, tiled=True)]
    all_to_all x2 -> x0, waiting for transfers between devices: 9.77 us -> none  [the longest x1 5.03 us: local(): lax.all_to_all(blocks, 'layer', split_axis=2, concat_axis=0, tiled=True)]
    reshape x5 -> x0, local copies, waits for them, and re-layouts: 3.21 us -> none  [the longest x2 1.74 us: local(): blocks = store.reshape(1, ex_dev, layers, width)]
    unnamed x9, local copies, waits for them, and re-layouts: 1.32 us -> 3.81 us
  transfers between devices with their start and end apart: 2 -> 0, of which waited for: 2 -> 0; matrix products, arithmetic and copies ran while one was open for 4% -> 0% of each run, Pallas kernels for 0% -> 0%
where the time goes in v1:
time: 20.9 us; the launch traced here: 20.7 us
  Pallas kernels  16.9 us (81%)
  local copies, waits for them, and re-layouts  3.81 us (18%)
    pallas_call x1, Pallas kernels, local(): pl.pallas_call(functools.partial(kernel, n), out_shape=jax.ShapeDtypeStru...  16.9 us
    unnamed x9, local copies, waits for them, and re-layouts  3.81 us

profile of v1, /device:TPU:0, one launch (start us, length us, event | category | flops | bytes accessed | tf_op | source)
XLA Modules:
  0.0 20.7 jit_solution(14880070917490936264)
XLA Ops:
  0.0 0.0 copy-start
  0.0 0.9 %copy-done = bf16[64,2,1024]{2,1,0:T(2,128)(2,1)S(1)} copy-done((bf16[64,2,1024]{2,1,0:T(2,128)(2,1)S(1)}, bf16[64,2,1024]{2,1,0:T(2,128)(2,1)}, u32[]{:S(2)}) %copy-start) | copy-done | bytes 262168
  1.0 0.0 copy-start.1
  1.0 0.9 %copy-done.1 = bf16[2,32,1024]{2,1,0:T(8,128)(2,1)S(1)} copy-done((bf16[2,32,1024]{2,1,0:T(8,128)(2,1)S(1)}, bf16[2,32,1024]{2,1,0:T(8,128)(2,1)}, u32[]{:S(2)}) %copy-start.1) | copy-done | bytes 131096
  1.9 0.0 copy-start.2
  1.9 0.7 %copy-done.2 = f32[2,1024]{1,0:T(2,128)S(1)} copy-done((f32[2,1024]{1,0:T(2,128)S(1)}, f32[2,1024]{1,0:T(2,128)}, u32[]{:S(2)}) %copy-start.2) | copy-done | bytes 8216
  2.6 0.0 copy-start.3
  2.6 0.7 %copy-done.3 = s32[2,32]{1,0:T(2,128)S(1)} copy-done((s32[2,32]{1,0:T(2,128)S(1)}, s32[2,32]{1,0:T(2,128)}, u32[]{:S(2)}) %copy-start.3) | copy-done | bytes 280
  3.2 16.9 %shard_map.46 = f32[4,32]{1,0:T(4,128)S(1)} custom-call(bf16[64,2,1024]{2,1,0:T(2,128)(2,1)S(1)} %copy-done, f32[2,1024]{1,0:T(2,128)S(1)} %copy-done.2, bf16[2,32,1024]{2,1,0:T(8,128)(2,1)S(1)} %copy-done.1, s32[2,32]{1,0:T(2,128)S(1)} %copy-done.3), custom_call_target="tpu_custom_call" | custom-call | tf_op jit(solution)/shard_map/pallas_call | solution.py:204
  20.1 0.6 %copy.6 = f32[4,32]{1,0:T(4,128)} copy(f32[4,32]{1,0:T(4,128)S(1)} %shard_map.46) | data formatting | bytes 1024
Async XLA Ops:
  0.0 0.9 %copy-start = (bf16[64,2,1024]{2,1,0:T(2,128)(2,1)S(1)}, bf16[64,2,1024]{2,1,0:T(2,128)(2,1)}, u32[]{:S(2)}) copy-start(bf16[64,2,1024]{2,1,0:T(2,128)(2,1)} %q_hbm.1) | copy-start | bytes 786436
  1.0 0.9 %copy-start.1 = (bf16[2,32,1024]{2,1,0:T(8,128)(2,1)S(1)}, bf16[2,32,1024]{2,1,0:T(8,128)(2,1)}, u32[]{:S(2)}) copy-start(bf16[2,32,1024]{2,1,0:T(8,128)(2,1)} %st_hbm.1) | copy-start | bytes 393220
  1.9 0.7 %copy-start.2 = (f32[2,1024]{1,0:T(2,128)S(1)}, f32[2,1024]{1,0:T(2,128)}, u32[]{:S(2)}) copy-start(f32[2,1024]{1,0:T(2,128)} %cur_hbm.1) | copy-start | bytes 24580
  2.6 0.7 %copy-start.3 = (s32[2,32]{1,0:T(2,128)S(1)}, s32[2,32]{1,0:T(2,128)}, u32[]{:S(2)}) copy-start(s32[2,32]{1,0:T(2,128)} %exp_hbm.1) | copy-start | bytes 772

commit v2 on v1

--- a/solution.py
+++ b/solution.py
@@ -68,11 +68,23 @@
     for load in loads:
         load.start()
 
+    def peer_of(k):
+        if n & (n - 1):
+            return lax.rem(me + k, n)
+        step = n - k
+        peer = me
+        bit = 1
+        while bit < n:
+            flip = step // bit % 2
+            peer = peer + flip * bit * (1 - 2 * lax.rem(me // bit, 2))
+            bit *= 2
+        return peer
+
     barrier = pltpu.get_barrier_semaphore()
 
     def greet(k):
         pl.semaphore_signal(
-            barrier, inc=1, device_id={"layer": lax.rem(me + k, n)}, device_id_type=MESH
+            barrier, inc=1, device_id={"layer": peer_of(k)}, device_id_type=MESH
         )
 
     each(1, n, greet)
@@ -119,9 +131,6 @@
             device_id={"layer": peer},
             device_id_type=MESH,
         )
-
-    def peer_of(k):
-        return lax.rem(me + k, n)
 
     each(1, n, lambda k: block_copy(peer_of(k), me).start())
     recv[me] = send[me]
@@ -203,7 +212,7 @@
         lanes = -(-2 * total // 128) * 128
         return pl.pallas_call(
             functools.partial(kernel, n),
-            out_shape=jax.ShapeDtypeStruct((own_q, total), jnp.float32),
+            out_shape=pltpu.VMEM((own_q, total), jnp.float32),
             in_specs=[pl.BlockSpec(memory_space=pl.ANY)] * 4,
             out_specs=pl.BlockSpec(memory_space=pltpu.VMEM),
             scratch_shapes=[
@@ -224,7 +233,7 @@
                 pltpu.SemaphoreType.DMA((n,)),
             ],
             compiler_params=pltpu.CompilerParams(
-                collective_id=0, has_side_effects=True, vmem_limit_bytes=32 * 1024 * 1024
+                collective_id=0, has_side_effects=True
             ),
         )(queries, inverse_curvature, store, exponents)
 

time: 20.9 us -> 16.9 us (0.81)
  local copies, waits for them, and re-layouts: 3.81 us -> 0.58 us
  Pallas kernels: 16.9 us -> 16.2 us
    unnamed x9 -> x1, local copies, waits for them, and re-layouts: 3.81 us -> 0.58 us
    pallas_call x1, Pallas kernels: 16.9 us -> 16.2 us  [local(): pl.pallas_call(functools.partial(kernel, n), out_shape=pltpu.VMEM((own_q,...]
where the time goes in v2:
time: 16.9 us; the launch traced here: 16.7 us
  Pallas kernels  16.2 us (96%)
  local copies, waits for them, and re-layouts  0.58 us (3%)
    pallas_call x1, Pallas kernels, local(): pl.pallas_call(functools.partial(kernel, n), out_shape=pltpu.VMEM((own_q,...  16.2 us
    unnamed x1, local copies, waits for them, and re-layouts  0.58 us

profile of v2, /device:TPU:0, one launch (start us, length us, event | category | flops | bytes accessed | tf_op | source)
XLA Modules:
  0.0 16.7 jit_solution(17631313080821202286)
XLA Ops:
  0.0 16.2 %shard_map.46 = f32[4,32]{1,0:T(4,128)S(1)} custom-call(bf16[64,2,1024]{2,1,0:T(2,128)(2,1)} %q_hbm.1, f32[2,1024]{1,0:T(2,128)} %cur_hbm.1, bf16[2,32,1024]{2,1,0:T(8,128)(2,1)} %st_hbm.1, s32[2,32]{1,0:T(2,128)} %exp_hbm.1), custom_call_target="tpu_custom_call" | custom-call | tf_op jit(solution)/shard_map/pallas_call | solution.py:213
  16.2 0.6 %copy.6 = f32[4,32]{1,0:T(4,128)} copy(f32[4,32]{1,0:T(4,128)S(1)} %shard_map.46) | data formatting | bytes 1024

commit v3 on v2

--- a/solution.py
+++ b/solution.py
@@ -41,6 +41,7 @@
     send,
     recv,
     weighted,
+    fold,
     part_send,
     part_recv,
     load_sem,
@@ -59,15 +60,6 @@
     own_q = count_q // n
     lanes = part_send.shape[2]
 
-    loads = [
-        pltpu.make_async_copy(src, dst, load_sem.at[i])
-        for i, (src, dst) in enumerate(
-            [(exp_hbm, exp_ref), (st_hbm, st_ref), (cur_hbm, cur_ref), (q_hbm, q_ref)]
-        )
-    ]
-    for load in loads:
-        load.start()
-
     def peer_of(k):
         if n & (n - 1):
             return lax.rem(me + k, n)
@@ -88,6 +80,15 @@
         )
 
     each(1, n, greet)
+
+    loads = [
+        pltpu.make_async_copy(src, dst, load_sem.at[i])
+        for i, (src, dst) in enumerate(
+            [(exp_hbm, exp_ref), (st_hbm, st_ref), (cur_hbm, cur_ref), (q_hbm, q_ref)]
+        )
+    ]
+    for load in loads:
+        load.start()
 
     loads[0].wait()
     loads[1].wait()
@@ -150,9 +151,19 @@
         rows = pl.ds(b * QBLOCK, QBLOCK)
         grid = q_ref[rows].astype(jnp.float32) * cur_ref[...][None]
         for m in range(mat_dev):
-            weighted[m, rows, :] = grid[:, m, :].astype(jnp.bfloat16)
+            plane = grid[:, m, :].astype(jnp.bfloat16)
+            for c in range(chunks):
+                at = pl.ds((m * chunks + c) * QBLOCK, QBLOCK)
+                weighted[b, at, :] = plane[:, c * depth : (c + 1) * depth]
 
     each(0, count_q // QBLOCK, weigh)
+
+    for first in range(0, n, SBLOCK):
+        size = min(SBLOCK, n - first)
+        source = iota((size * ROWS, lanes), 0)
+        owner = (first + source // ROWS) * ex + lax.rem(source, sub) // chunks
+        ones = jnp.where(owner == iota((size * ROWS, lanes), 1), 1.0, 0.0)
+        fold[pl.ds(first * ROWS, size * ROWS), :] = ones.astype(jnp.bfloat16)
 
     each(1, n, lambda k: block_copy(peer_of(k), peer_of(k)).wait_recv())
 
@@ -163,27 +174,28 @@
             size = min(SBLOCK, n - first)
             width = size * ROWS
             blocks = recv[pl.ds(first, size)].reshape(width, depth)
-            place = lax.rem(iota((QBLOCK, width), 1), ROWS)
-            mix = jnp.zeros((QBLOCK, width), jnp.float32)
-            for m in range(mat_dev):
-                for c in range(chunks):
-                    product = lax.dot_general(
-                        weighted[m, rows, pl.ds(c * depth, depth)],
-                        blocks,
-                        (((1,), (1,)), ((), ())),
-                        preferred_element_type=jnp.float32,
-                    )
-                    mine = (place // sub == m) & (lax.rem(place, chunks) == c)
-                    mix = jnp.where(mine, product, mix)
+            products = lax.dot_general(
+                weighted[b], blocks, (((1,), (1,)), ((), ())), preferred_element_type=jnp.float32
+            )
+            kept = [products[i * QBLOCK : (i + 1) * QBLOCK] for i in range(mat_dev * chunks)]
+            place = iota((QBLOCK, width), 1)
+            bit = 1
+            while len(kept) > 1:
+                odd = jnp.bitwise_and(place, bit) != 0
+                kept = [jnp.where(odd, kept[i + 1], kept[i]) for i in range(0, len(kept), 2)]
+                bit *= 2
+                if bit == chunks:
+                    bit = sub
+            mix = kept[0]
             high = mix.astype(jnp.bfloat16)
             rest = mix - high.astype(jnp.float32)
-            middle = rest.astype(jnp.bfloat16)
-            low = (rest - middle.astype(jnp.float32)).astype(jnp.bfloat16)
-            source = iota((width, lanes), 0)
-            owner = (first + source // ROWS) * ex + lax.rem(source, sub) // chunks
-            fold = jnp.where(owner == iota((width, lanes), 1), 1.0, 0.0).astype(jnp.bfloat16)
-            for piece in (low, middle, high):
-                result = result + jnp.dot(piece, fold, preferred_element_type=jnp.float32)
+            low = rest.astype(jnp.bfloat16)
+            pieces = jnp.dot(
+                jnp.concatenate([high, low], axis=0),
+                fold[pl.ds(first * ROWS, width), :],
+                preferred_element_type=jnp.float32,
+            )
+            result = result + (pieces[QBLOCK:] + pieces[:QBLOCK])
         for j in range(QBLOCK // own_q):
             part_send[b * (QBLOCK // own_q) + j] = result[j * own_q : (j + 1) * own_q, :]
 
@@ -223,7 +235,8 @@
                 pltpu.VMEM((depth // 128, n * ROWS, 128), jnp.float32),
                 pltpu.VMEM((n, ROWS, depth), jnp.bfloat16),
                 pltpu.VMEM((n, ROWS, depth), jnp.bfloat16),
-                pltpu.VMEM((mat_dev, count_q, feat), jnp.bfloat16),
+                pltpu.VMEM((count_q // QBLOCK, QBLOCK * mat_dev * chunks, depth), jnp.bfloat16),
+                pltpu.VMEM((n * ROWS, lanes), jnp.bfloat16),
                 pltpu.VMEM((n, own_q, lanes), jnp.float32),
                 pltpu.VMEM((n, own_q, lanes), jnp.float32),
                 pltpu.SemaphoreType.DMA((4,)),

time: 16.9 us -> 16.7 us (0.988)
  Pallas kernels: 16.2 us -> 16 us
where the time goes in v3:
time: 16.7 us; the launch traced here: 16.6 us
  Pallas kernels  16 us (96%)
  local copies, waits for them, and re-layouts  0.58 us (3%)
    pallas_call x1, Pallas kernels, local(): pl.pallas_call(functools.partial(kernel, n), out_shape=pltpu.VMEM((own_q,...  16 us
    unnamed x1, local copies, waits for them, and re-layouts  0.58 us

profile of v3, /device:TPU:0, one launch (start us, length us, event | category | flops | bytes accessed | tf_op | source)
XLA Modules:
  0.0 16.6 jit_solution(12831298861778814621)
XLA Ops:
  0.0 16.0 %shard_map.46 = f32[4,32]{1,0:T(4,128)S(1)} custom-call(bf16[64,2,1024]{2,1,0:T(2,128)(2,1)} %q_hbm.1, f32[2,1024]{1,0:T(2,128)} %cur_hbm.1, bf16[2,32,1024]{2,1,0:T(8,128)(2,1)} %st_hbm.1, s32[2,32]{1,0:T(2,128)} %exp_hbm.1), custom_call_target="tpu_custom_call" | custom-call | tf_op jit(solution)/shard_map/pallas_call | solution.py:225
  16.0 0.6 %copy.6 = f32[4,32]{1,0:T(4,128)} copy(f32[4,32]{1,0:T(4,128)S(1)} %shard_map.46) | data formatting | bytes 1024

commit v4 on v3

--- a/solution.py
+++ b/solution.py
@@ -117,8 +117,8 @@
         return pltpu.make_async_remote_copy(
             src_ref=send.at[peer],
             dst_ref=recv.at[slot],
-            send_sem=send_sem.at[peer],
-            recv_sem=recv_sem.at[slot],
+            send_sem=send_sem,
+            recv_sem=recv_sem,
             device_id={"layer": peer},
             device_id_type=MESH,
         )
@@ -127,9 +127,20 @@
         return pltpu.make_async_remote_copy(
             src_ref=part_send.at[peer],
             dst_ref=part_recv.at[slot],
-            send_sem=psend_sem.at[peer],
-            recv_sem=precv_sem.at[slot],
+            send_sem=psend_sem,
+            recv_sem=precv_sem,
             device_id={"layer": peer},
+            device_id_type=MESH,
+        )
+
+    def all_of(src, dst, sent, received):
+        most = pl.ds(0, n - 1)
+        return pltpu.make_async_remote_copy(
+            src_ref=src.at[most],
+            dst_ref=dst.at[most],
+            send_sem=sent,
+            recv_sem=received,
+            device_id={"layer": peer_of(1)},
             device_id_type=MESH,
         )
 
@@ -165,7 +176,7 @@
         ones = jnp.where(owner == iota((size * ROWS, lanes), 1), 1.0, 0.0)
         fold[pl.ds(first * ROWS, size * ROWS), :] = ones.astype(jnp.bfloat16)
 
-    each(1, n, lambda k: block_copy(peer_of(k), peer_of(k)).wait_recv())
+    all_of(send, recv, send_sem, recv_sem).wait_recv()
 
     def score(b):
         rows = pl.ds(b * QBLOCK, QBLOCK)
@@ -203,12 +214,12 @@
 
     each(1, n, lambda k: part_copy(peer_of(k), me).start())
     part_recv[me] = part_send[me]
-    each(1, n, lambda k: part_copy(peer_of(k), peer_of(k)).wait_recv())
+    all_of(part_send, part_recv, psend_sem, precv_sem).wait_recv()
     final = jnp.sum(part_recv[...], axis=0)
     out_ref[...] = final[:, :total] / jnp.sqrt(final[:, total : 2 * total] + 1e-06)
 
-    each(1, n, lambda k: block_copy(peer_of(k), me).wait_send())
-    each(1, n, lambda k: part_copy(peer_of(k), me).wait_send())
+    all_of(send, recv, send_sem, recv_sem).wait_send()
+    all_of(part_send, part_recv, psend_sem, precv_sem).wait_send()
 
 
 def solution(mesh):
@@ -240,10 +251,10 @@
                 pltpu.VMEM((n, own_q, lanes), jnp.float32),
                 pltpu.VMEM((n, own_q, lanes), jnp.float32),
                 pltpu.SemaphoreType.DMA((4,)),
-                pltpu.SemaphoreType.DMA((n,)),
-                pltpu.SemaphoreType.DMA((n,)),
-                pltpu.SemaphoreType.DMA((n,)),
-                pltpu.SemaphoreType.DMA((n,)),
+                pltpu.SemaphoreType.DMA(()),
+                pltpu.SemaphoreType.DMA(()),
+                pltpu.SemaphoreType.DMA(()),
+                pltpu.SemaphoreType.DMA(()),
             ],
             compiler_params=pltpu.CompilerParams(
                 collective_id=0, has_side_effects=True

time: 16.7 us -> 16.1 us (0.964)
  Pallas kernels: 16 us -> 15.4 us
    pallas_call x1, Pallas kernels: 16 us -> 15.4 us  [local(): pl.pallas_call(functools.partial(kernel, n), out_shape=pltpu.VMEM((own_q,...]
where the time goes in v4:
time: 16.1 us; the launch traced here: 16 us
  Pallas kernels  15.4 us (96%)
  local copies, waits for them, and re-layouts  0.58 us (4%)
    pallas_call x1, Pallas kernels, local(): pl.pallas_call(functools.partial(kernel, n), out_shape=pltpu.VMEM((own_q,...  15.4 us
    unnamed x1, local copies, waits for them, and re-layouts  0.58 us

profile of v4, /device:TPU:0, one launch (start us, length us, event | category | flops | bytes accessed | tf_op | source)
XLA Modules:
  0.0 16.0 jit_solution(1179761322209468307)
XLA Ops:
  0.0 15.4 %shard_map.46 = f32[4,32]{1,0:T(4,128)S(1)} custom-call(bf16[64,2,1024]{2,1,0:T(2,128)(2,1)} %q_hbm.1, f32[2,1024]{1,0:T(2,128)} %cur_hbm.1, bf16[2,32,1024]{2,1,0:T(8,128)(2,1)} %st_hbm.1, s32[2,32]{1,0:T(2,128)} %exp_hbm.1), custom_call_target="tpu_custom_call" | custom-call | tf_op jit(solution)/shard_map/pallas_call | solution.py:236
  15.4 0.6 %copy.6 = f32[4,32]{1,0:T(4,128)} copy(f32[4,32]{1,0:T(4,128)S(1)} %shard_map.46) | data formatting | bytes 1024
